TPU v7x, 32 devices: a whole 2x2x4 slice. The times are simulated.
32 devices in a mesh: row: 8 (over y, x, core), col: 4 (over z).
Axes of the slice: x: 2, y: 2, z: 4, core: 2. Of those that a mesh axis runs over, the one named last changes fastest.
Arguments:
- mask: float32 [4096, 2048], P('row', 'col'), may hold values from -1 to 1
- row_taps: float32 [24, 65], replicated, may hold values from -0.75 to 0.75
- col_taps: float32 [24, 65], replicated, may hold values from -0.75 to 0.75
- kernel_weights: float32 [24], replicated, may hold values from 0.1 to 1
- target: float32 [4096, 2048], P('row', 'col'), may hold values from 0 to 1
- density: int32 [8, 4], P('row', 'col'), may hold values from 0 to 2
Outputs:
- resist: float32 [4096, 2048], P('row', 'col')
- gradient: float32 [4096, 2048], P('row', 'col')
All inputs are finite; a program needn't handle non-finite values.
Results may differ from a plain program's by a relative error of at most 0.0003.
Values sent between devices are 32-bit elements; how exact they have to be, the bound alone decides.
A program may use at most 192 MiB of HBM per device.

v0:
```python
import jax
import jax.numpy as jnp
from jax import lax
from jax.sharding import PartitionSpec as P

resist_slope = 6.0
resist_level = 0.33


def padded(block, sides, width):
    for axis, dim in sides:
        count = lax.axis_size(axis)
        forward = [(i, i + 1) for i in range(count - 1)]
        backward = [(target, source) for source, target in forward]
        low = lax.ppermute(
            lax.slice_in_dim(block, block.shape[dim] - width, None, axis=dim), axis, forward
        )
        high = lax.ppermute(lax.slice_in_dim(block, 0, width, axis=dim), axis, backward)
        block = jnp.concatenate([low, block, high], axis=dim)
    return block


def band_tables(taps, block_len):
    span = taps.shape[1]
    out_index = jnp.arange(block_len)[:, None, None]
    in_index = jnp.arange(block_len + span - 1)[None, :, None]
    tap_index = jnp.arange(span)[None, None, :]
    onehot = (in_index - out_index == tap_index).astype(jnp.float32)
    return jnp.einsum("kp,ijp->kij", taps, onehot, precision=lax.Precision.HIGHEST)


def stack_rows(extended, block_len, reach, axis):
    count_blocks = (extended.shape[axis] - 2 * reach) // block_len
    return jnp.stack(
        [
            lax.slice_in_dim(
                extended, number * block_len, number * block_len + block_len + 2 * reach, 1, axis
            )
            for number in range(count_blocks)
        ],
        axis=axis,
    )


def correlate(stacked, row_table, col_table, reach):
    groups = row_table.shape[0]
    if stacked.ndim == 3:
        row_pass = jnp.einsum("gij,bjc->gbic", row_table, stacked, precision=lax.Precision.HIGHEST)
    else:
        row_pass = jnp.einsum("gij,gbjc->gbic", row_table, stacked, precision=lax.Precision.HIGHEST)
    row_pass = row_pass.reshape(groups, -1, row_pass.shape[3])
    col_len = col_table.shape[1]
    count_cols = (row_pass.shape[2] - 2 * reach) // col_len
    col_blocks = jnp.stack(
        [
            row_pass[:, :, number * col_len : number * col_len + col_len + 2 * reach]
            for number in range(count_cols)
        ],
        axis=1,
    )
    result = jnp.einsum("gcrj,gij->grci", col_blocks, col_table, precision=lax.Precision.HIGHEST)
    return result.reshape(groups, result.shape[1], -1)


def shards(mask, row_taps, col_taps, kernel_weights, target, density):
    height, breadth = mask.shape
    kernels = row_taps.shape[0]
    kstep = kernels // 3
    reach = (row_taps.shape[1] - 1) // 2
    row_len = min(height, 128)
    col_len = min(breadth, 128)
    row_tables = band_tables(row_taps, row_len)
    col_tables = band_tables(col_taps, col_len)
    active_groups = density[0, 0] + 1
    active_count = kstep * active_groups
    active = (jnp.arange(kernels) < active_count).astype(jnp.float32)
    weight_sum = jnp.sum(kernel_weights * active)
    extended = padded(mask, (("row", 0), ("col", 1)), reach)
    stacked = stack_rows(extended, row_len, reach, 0)

    def forward_step(group, carry):
        fields, intensity = carry
        first = group * kstep
        row_group = lax.dynamic_slice_in_dim(row_tables, first, kstep, 0)
        col_group = lax.dynamic_slice_in_dim(col_tables, first, kstep, 0)
        weights = lax.dynamic_slice_in_dim(kernel_weights, first, kstep, 0)
        field = correlate(stacked, row_group, col_group, reach)
        fields = lax.dynamic_update_slice_in_dim(fields, field, first, 0)
        return (fields, intensity + jnp.sum(weights[:, None, None] * field * field, axis=0))

    start = (
        jnp.zeros((kernels, height, breadth), jnp.float32),
        jnp.zeros((height, breadth), jnp.float32),
    )
    fields, intensity = lax.fori_loop(0, active_groups, forward_step, start)
    intensity = intensity / weight_sum
    resist = jax.nn.sigmoid(resist_slope * (intensity - resist_level))
    error = (resist - target) * resist_slope * resist * (1.0 - resist)
    scaled = 2.0 * kernel_weights / weight_sum
    field_grads = scaled[:, None, None] * error[None] * fields
    grad_rims = padded(field_grads, (("row", 1), ("col", 2)), reach)
    flip_rows = band_tables(row_taps[:, ::-1], row_len)
    flip_cols = band_tables(col_taps[:, ::-1], col_len)

    def adjoint_step(group, gradient):
        first = group * kstep
        rim_group = lax.dynamic_slice_in_dim(grad_rims, first, kstep, 0)
        piece = stack_rows(rim_group, row_len, reach, 1)
        row_group = lax.dynamic_slice_in_dim(flip_rows, first, kstep, 0)
        col_group = lax.dynamic_slice_in_dim(flip_cols, first, kstep, 0)
        return gradient + jnp.sum(correlate(piece, row_group, col_group, reach), axis=0)

    gradient = lax.fori_loop(0, 3, adjoint_step, jnp.zeros((height, breadth), jnp.float32))
    return (resist, gradient)


def solution(mesh):
    return jax.shard_map(
        shards,
        mesh=mesh,
        in_specs=(P("row", "col"), P(), P(), P(), P("row", "col"), P("row", "col")),
        out_specs=(P("row", "col"), P("row", "col")),
        check_vma=False,
    )
```

profile of v0, /device:TPU:3, one launch (start us, length us, event | category | flops | bytes accessed | tf_op | source)
XLA Modules:
  0.0 624.3 jit_solution(11697196859265340802)
XLA Ops:
  31.8 11.5 %broadcast_in_dim.2.clone = f32[24,512,512]{2,1,0:T(8,128)} broadcast(f32[]{:T(128)} %constant.56.clone.1), dimensions={} | broadcast | bytes 25165828 | tf_op jit(solution)/shard_map/broadcast_in_dim | solution.py:92
  44.4 117.3 %while.26 = (s32[]{:T(128)}, f32[24,512,512]{2,1,0:T(8,128)}, f32[512,512]{0,1:T(8,128)}, s32[]{:T(128)}, f32[24,128,192]{1,0,2:T(8,128)}, /*index=5*/f32[24,128...) while((s32[]{:T(128)}, f32[24,512,512]{2,1,0:T(8,128)}, ...), condition=%wide.region_2.3_spmd, body=%wide.region_0.2_spmd.sunk | while | flops 10283384832 | bytes 145424816 | solution.py:95
  70.0 14.7 %fusion.59 = (f32[512,4,128]{0,2,1:T(8,128)}, f32[8,128,4,512]{3,1,2,0:T(8,128)}) fusion(f32[8]{0:T(128)S(1)} %dynamic_slice.41, f32[8,1,512,192]{2,3,1,0:T(8,128)S(1)} %get-tuple-element.374, f32[8,1,512,192]{2,3,1,0:T(8,128)} %get-tuple-element.375, f32[8,1,512,192]{2,3,1,0:T(8,128)} %get-tuple-element.376, ...), kind=kOutput, calls=%fused_computation.10.clone.1 | convolution fusion | flops 4847304704 | bytes 22806560 | tf_op jit(solution)/shard_map/while/body/gcrj,gij->grci/dot_general | solution.py:61
  84.7 9.1 %copy.97 = f32[8,512,512]{2,1,0:T(8,128)} copy(f32[8,512,512]{1,2,0:T(8,128)} %bitcast.141) | data formatting | bytes 16777216 | tf_op jit(solution)/shard_map/while/body/dynamic_update_slice | solution.py:88
  128.4 14.7 %fusion.59 = (f32[512,4,128]{0,2,1:T(8,128)}, f32[8,128,4,512]{3,1,2,0:T(8,128)}) fusion(f32[8]{0:T(128)S(1)} %dynamic_slice.41, f32[8,1,512,192]{2,3,1,0:T(8,128)S(1)} %get-tuple-element.374, f32[8,1,512,192]{2,3,1,0:T(8,128)} %get-tuple-element.375, f32[8,1,512,192]{2,3,1,0:T(8,128)} %get-tuple-element.376, ...), kind=kOutput, calls=%fused_computation.10.clone.1 | convolution fusion | flops 4847304704 | bytes 22806560 | tf_op jit(solution)/shard_map/while/body/gcrj,gij->grci/dot_general | solution.py:61
  143.1 9.1 %copy.97 = f32[8,512,512]{2,1,0:T(8,128)} copy(f32[8,512,512]{1,2,0:T(8,128)} %bitcast.141) | data formatting | bytes 16777216 | tf_op jit(solution)/shard_map/while/body/dynamic_update_slice | solution.py:88
  166.5 10.7 %multiply_multiply_fusion.1 = f32[24,512,512]{2,1,0:T(8,128)S(1)} fusion(f32[24,512,512]{2,1,0:T(8,128)} %get-tuple-element.141, f32[512,512]{1,0:T(8,128)S(1)} %get-tuple-element.247, f32[24]{0:T(128)S(1)} %copy-done.11), kind=kLoop, calls=%fused_computation.58 | loop fusion | flops 12582912 | bytes 51380320 | tf_op jit(solution)/shard_map/mul | solution.py:100
  192.7 15.4 %collective-permute-done.4 = f32[24,32,512]{2,1,0:T(8,128)S(1)} collective-permute-done((f32[24,32,512]{2,1,0:T(8,128)S(1)}, f32[24,32,512]{2,1,0:T(8,128)S(1)}, u32[]{:S(2)}, u32[]{:S(2)}) %collective-permute-start.4) | collective-permute-done | bytes 1572896 | tf_op jit(solution)/shard_map/ppermute | solution.py:15
  213.4 9.6 %pad_maximum_fusion.3 = (f32[24,576,32]{2,1,0:T(8,128)}, f32[24,576,32]{2,1,0:T(8,128)}) fusion(f32[24,32,512]{2,1,0:T(8,128)S(1)} %collective-permute-done.5, f32[24,512,512]{2,1,0:T(8,128)} %copy-done, f32[24,32,512]{2,1,0:T(8,128)S(1)} %collective-permute-done.4), kind=kLoop, calls=%fused_computation.61 | loop fusion | flops 1769472 | bytes 31850496 | tf_op jit(solution)/shard_map/slice | solution.py:16
  229.1 75.0 %collective-permute-start.6 = (f32[24,576,32]{1,2,0:T(8,128)}, f32[24,576,32]{1,2,0:T(8,128)}, u32[]{:S(2)}, u32[]{:S(2)}) collective-permute-start(f32[24,576,32]{1,2,0:T(8,128)} %copy.53), channel_id=1, source_target_pairs={{0,1},{1,2},{2,3},{4,5},{5,6},{6,7},{8,9},{9,10},{10,11},{12,13},{... | collective-permute-start | bytes 5308424 | tf_op jit(solution)/shard_map/ppermute | solution.py:15
  319.7 23.4 %collective-permute-done.6 = f32[24,576,32]{1,2,0:T(8,128)} collective-permute-done((f32[24,576,32]{1,2,0:T(8,128)}, f32[24,576,32]{1,2,0:T(8,128)}, u32[]{:S(2)}, u32[]{:S(2)}) %collective-permute-start.6) | collective-permute-done | bytes 1769504 | tf_op jit(solution)/shard_map/ppermute | solution.py:15
  360.0 33.1 %pad_maximum_fusion = f32[24,576,576]{2,1,0:T(8,128)} fusion(f32[24,576,32]{2,1,0:T(8,128)} %copy.56, f32[24,32,512]{2,1,0:T(8,128)S(1)} %collective-permute-done.5, f32[24,512,512]{2,1,0:T(8,128)} %copy-done, f32[24,32,512]{2,1,0:T(8,128)S(1)} %collective-permute-done.4, f32[24,576,32]{2,1,0:T(8,128)} %copy.55), kind=kLoop, calls=%fused_computation.57 | loop fusion | flops 31850496 | bytes 63700992 | tf_op jit(solution)/shard_map/concatenate | solution.py:19
  393.0 228.4 %while.27 = (s32[]{:T(128)}, f32[512,512]{0,1:T(8,128)}, f32[24,128,192]{1,0,2:T(8,128)}, f32[24,576,576]{2,1,0:T(8,128)}, f32[24,128,192]{1,0,2:T(8,128)}, /*in...) while((s32[]{:T(128)}, f32[512,512]{0,1:T(8,128)}, ...), condition=%wide.region_5.6_spmd.clone, body=%wide.region_4.5_spmd.clone.sunk | while | flops 10288234496 | bytes 117440736 | solution.py:113
  393.2 11.4 %dynamic-slice_bitcast_fusion.5 = (f32[8,1,192,576]{3,2,1,0:T(8,128)}, f32[8,1,192,576]{3,2,1,0:T(8,128)}, f32[8,1,192,576]{3,2,1,0:T(8,128)}, f32[8,1,192,576]{3,2,1,0:T(8,128)}) fusion(f32[24,576,576]{2,1,0:T(8,128)} %get-tuple-element.459, s32[]{:T(128)S(6)} %select_n.19, s32[]{:T(128)S(6)} %add.82, s32[]{:T(128)S(6)} %add.83, s32[]{:T(128)S(6)} %add.84), kind=kLoop, calls=%fused_computation.44.clone.1 | loop fusion | bytes 28311568 | tf_op jit(solution)/shard_map/while/body/eval_jaxpr/stack | solution.py:34
  407.0 35.5 %fusion.62 = f32[8,4,72,8,128]{4,3,2,1,0:T(8,128)S(1)} fusion(f32[8,1,192,576]{3,2,1,0:T(8,128)} %get-tuple-element.386, f32[8,1,192,576]{3,2,1,0:T(8,128)} %get-tuple-element.387, f32[8,1,192,576]{3,2,1,0:T(8,128)} %get-tuple-element.388, f32[8,1,192,576]{3,2,1,0:T(8,128)} %get-tuple-element.389, f32[8,128,192]{1,0,2:T(8,128)S(1)} %get-tuple-element.390), kind=kOutput, calls=%fused_computation.45.clone.1 | convolution fusion | flops 5446434816 | bytes 24379392 | tf_op jit(solution)/shard_map/while/body/eval_jaxpr/gij,gbjc->gbic/dot_general | solution.py:50
  447.4 9.1 %slice_bitcast_fusion.15 = (f32[8,1,512,192]{2,3,0,1:T(8,128)S(1)}, f32[8,1,512,192]{2,3,0,1:T(8,128)S(1)}, f32[8,1,512,192]{2,3,0,1:T(8,128)}, f32[8,1,512,192]{2,3,0,1:T(8,128)}) fusion(f32[8,512,576]{1,2,0:T(8,128)} %bitcast.140), kind=kLoop, calls=%fused_computation.49.clone.1 | loop fusion | bytes 25165824 | tf_op jit(solution)/shard_map/while/body/eval_jaxpr/stack | solution.py:54
  456.5 10.1 %fusion.63 = f32[128,4,512,1]{2,0,3,1:T(8,128)} fusion(f32[8,1,512,192]{2,3,0,1:T(8,128)S(1)} %get-tuple-element.391, f32[8,1,512,192]{2,3,0,1:T(8,128)} %get-tuple-element.392, f32[8,1,512,192]{2,3,0,1:T(8,128)} %get-tuple-element.393, f32[8,1,512,192]{2,3,0,1:T(8,128)S(1)} %get-tuple-element.394, f32[8,128,192]{1,0,2:T(8,128)} %get-tuple-element.395), kind=kOutput, calls=%fused_computation.32.clone.1 | convolution fusion | flops 4841275392 | bytes 14417920 | tf_op jit(solution)/shard_map/while/body/eval_jaxpr/gcrj,gij->grci/dot_general | solution.py:61
  469.1 11.4 %dynamic-slice_bitcast_fusion.5 = (f32[8,1,192,576]{3,2,1,0:T(8,128)}, f32[8,1,192,576]{3,2,1,0:T(8,128)}, f32[8,1,192,576]{3,2,1,0:T(8,128)}, f32[8,1,192,576]{3,2,1,0:T(8,128)}) fusion(f32[24,576,576]{2,1,0:T(8,128)} %get-tuple-element.459, s32[]{:T(128)S(6)} %select_n.19, s32[]{:T(128)S(6)} %add.82, s32[]{:T(128)S(6)} %add.83, s32[]{:T(128)S(6)} %add.84), kind=kLoop, calls=%fused_computation.44.clone.1 | loop fusion | bytes 28311568 | tf_op jit(solution)/shard_map/while/body/eval_jaxpr/stack | solution.py:34
  482.9 35.5 %fusion.62 = f32[8,4,72,8,128]{4,3,2,1,0:T(8,128)S(1)} fusion(f32[8,1,192,576]{3,2,1,0:T(8,128)} %get-tuple-element.386, f32[8,1,192,576]{3,2,1,0:T(8,128)} %get-tuple-element.387, f32[8,1,192,576]{3,2,1,0:T(8,128)} %get-tuple-element.388, f32[8,1,192,576]{3,2,1,0:T(8,128)} %get-tuple-element.389, f32[8,128,192]{1,0,2:T(8,128)S(1)} %get-tuple-element.390), kind=kOutput, calls=%fused_computation.45.clone.1 | convolution fusion | flops 5446434816 | bytes 24379392 | tf_op jit(solution)/shard_map/while/body/eval_jaxpr/gij,gbjc->gbic/dot_general | solution.py:50
  523.3 9.1 %slice_bitcast_fusion.15 = (f32[8,1,512,192]{2,3,0,1:T(8,128)S(1)}, f32[8,1,512,192]{2,3,0,1:T(8,128)S(1)}, f32[8,1,512,192]{2,3,0,1:T(8,128)}, f32[8,1,512,192]{2,3,0,1:T(8,128)}) fusion(f32[8,512,576]{1,2,0:T(8,128)} %bitcast.140), kind=kLoop, calls=%fused_computation.49.clone.1 | loop fusion | bytes 25165824 | tf_op jit(solution)/shard_map/while/body/eval_jaxpr/stack | solution.py:54
  532.3 10.1 %fusion.63 = f32[128,4,512,1]{2,0,3,1:T(8,128)} fusion(f32[8,1,512,192]{2,3,0,1:T(8,128)S(1)} %get-tuple-element.391, f32[8,1,512,192]{2,3,0,1:T(8,128)} %get-tuple-element.392, f32[8,1,512,192]{2,3,0,1:T(8,128)} %get-tuple-element.393, f32[8,1,512,192]{2,3,0,1:T(8,128)S(1)} %get-tuple-element.394, f32[8,128,192]{1,0,2:T(8,128)} %get-tuple-element.395), kind=kOutput, calls=%fused_computation.32.clone.1 | convolution fusion | flops 4841275392 | bytes 14417920 | tf_op jit(solution)/shard_map/while/body/eval_jaxpr/gcrj,gij->grci/dot_general | solution.py:61
  545.3 11.4 %dynamic-slice_bitcast_fusion.5 = (f32[8,1,192,576]{3,2,1,0:T(8,128)}, f32[8,1,192,576]{3,2,1,0:T(8,128)}, f32[8,1,192,576]{3,2,1,0:T(8,128)}, f32[8,1,192,576]{3,2,1,0:T(8,128)}) fusion(f32[24,576,576]{2,1,0:T(8,128)} %get-tuple-element.459, s32[]{:T(128)S(6)} %select_n.19, s32[]{:T(128)S(6)} %add.82, s32[]{:T(128)S(6)} %add.83, s32[]{:T(128)S(6)} %add.84), kind=kLoop, calls=%fused_computation.44.clone.1 | loop fusion | bytes 28311568 | tf_op jit(solution)/shard_map/while/body/eval_jaxpr/stack | solution.py:34
  559.0 35.5 %fusion.62 = f32[8,4,72,8,128]{4,3,2,1,0:T(8,128)S(1)} fusion(f32[8,1,192,576]{3,2,1,0:T(8,128)} %get-tuple-element.386, f32[8,1,192,576]{3,2,1,0:T(8,128)} %get-tuple-element.387, f32[8,1,192,576]{3,2,1,0:T(8,128)} %get-tuple-element.388, f32[8,1,192,576]{3,2,1,0:T(8,128)} %get-tuple-element.389, f32[8,128,192]{1,0,2:T(8,128)S(1)} %get-tuple-element.390), kind=kOutput, calls=%fused_computation.45.clone.1 | convolution fusion | flops 5446434816 | bytes 24379392 | tf_op jit(solution)/shard_map/while/body/eval_jaxpr/gij,gbjc->gbic/dot_general | solution.py:50
  608.5 10.1 %fusion.63 = f32[128,4,512,1]{2,0,3,1:T(8,128)} fusion(f32[8,1,512,192]{2,3,0,1:T(8,128)S(1)} %get-tuple-element.391, f32[8,1,512,192]{2,3,0,1:T(8,128)} %get-tuple-element.392, f32[8,1,512,192]{2,3,0,1:T(8,128)} %get-tuple-element.393, f32[8,1,512,192]{2,3,0,1:T(8,128)S(1)} %get-tuple-element.394, f32[8,128,192]{1,0,2:T(8,128)} %get-tuple-element.395), kind=kOutput, calls=%fused_computation.32.clone.1 | convolution fusion | flops 4841275392 | bytes 14417920 | tf_op jit(solution)/shard_map/while/body/eval_jaxpr/gcrj,gij->grci/dot_general | solution.py:61
  (100 shorter events, 205.9 us)
Async XLA Ops:
  0.6 17.3 %copy-start.8 = (f32[512,512]{1,0:T(8,128)S(1)}, f32[512,512]{1,0:T(8,128)}, u32[]{:S(2)}) copy-start(f32[512,512]{1,0:T(8,128)} %param.10) | copy-start | bytes 3145732
  0.6 16.7 %copy-start.12 = (f32[24]{0:T(128)S(1)}, f32[24]{0:T(128)}, u32[]{:S(2)}) copy-start(f32[24]{0:T(128)} %param.13) | copy-start | bytes 292
  1.6 16.3 %collective-permute-start = (f32[32,512]{1,0:T(8,128)S(1)}, f32[32,512]{1,0:T(8,128)S(1)}, u32[]{:S(2)}, u32[]{:S(2)}) collective-permute-start(f32[32,512]{1,0:T(8,128)S(1)} %get-tuple-element.278), channel_id=1, source_target_pairs={{0,4},{4,8},{8,12},{12,16},{16,20},{20,24},{24,28},{1,5},{5,9},{9,... | collective-permute-start | bytes 196616 | tf_op jit(solution)/shard_map/ppermute | solution.py:15
  5.3 12.7 %collective-permute-start.1 = (f32[32,512]{1,0:T(8,128)S(1)}, f32[32,512]{1,0:T(8,128)S(1)}, u32[]{:S(2)}, u32[]{:S(2)}) collective-permute-start(f32[32,512]{1,0:T(8,128)S(1)} %get-tuple-element.277), channel_id=1, source_target_pairs={{4,0},{8,4},{12,8},{16,12},{20,16},{24,20},{28,24},{5,1},{9,5},{13... | collective-permute-start | bytes 196616 | tf_op jit(solution)/shard_map/ppermute | solution.py:18
  7.3 4.7 copy-start.6
  18.2 8.9 %collective-permute-start.2 = (f32[576,32]{1,0:T(8,128)S(1)}, f32[576,32]{1,0:T(8,128)S(1)}, u32[]{:S(2)}, u32[]{:S(2)}) collective-permute-start(f32[576,32]{1,0:T(8,128)S(1)} %get-tuple-element.275), channel_id=1, source_target_pairs={{0,1},{1,2},{2,3},{4,5},{5,6},{6,7},{8,9},{9,10},{10,11},{12,13},{... | collective-permute-start | bytes 221192 | tf_op jit(solution)/shard_map/ppermute | solution.py:15
  21.5 9.5 %collective-permute-start.3 = (f32[576,32]{1,0:T(8,128)S(1)}, f32[576,32]{1,0:T(8,128)S(1)}, u32[]{:S(2)}, u32[]{:S(2)}) collective-permute-start(f32[576,32]{1,0:T(8,128)S(1)} %get-tuple-element.276), channel_id=1, source_target_pairs={{1,0},{2,1},{3,2},{5,4},{6,5},{7,6},{9,8},{10,9},{11,10},{13,12},{... | collective-permute-start | bytes 221192 | tf_op jit(solution)/shard_map/ppermute | solution.py:18
  44.6 11.5 %copy-start.1 = (f32[4,192,576]{2,1,0:T(8,128)}, f32[4,192,576]{2,1,0:T(8,128)S(1)}, u32[]{:S(2)}) copy-start(f32[4,192,576]{2,1,0:T(8,128)S(1)} %get-tuple-element.426) | copy-start | bytes 5308420 | tf_op jit(solution)/shard_map/while
  93.9 7.8 %copy-start.3 = (f32[512,512]{0,1:T(8,128)S(1)}, f32[512,512]{0,1:T(8,128)}, u32[]{:S(2)}) copy-start(f32[512,512]{0,1:T(8,128)} %get-tuple-element.410) | copy-start | bytes 3145732 | tf_op jit(solution)/shard_map/while
  93.9 7.8 %copy-start.5 = (f32[512,4,128]{0,2,1:T(8,128)S(1)}, f32[512,4,128]{0,2,1:T(8,128)}, u32[]{:S(2)}) copy-start(f32[512,4,128]{0,2,1:T(8,128)} %get-tuple-element.380) | copy-start | bytes 3145732 | tf_op jit(solution)/shard_map/while
  93.9 9.1 %copy-start.2 = (f32[4,192,576]{2,1,0:T(8,128)S(1)}, f32[4,192,576]{2,1,0:T(8,128)}, u32[]{:S(2)}) copy-start(f32[4,192,576]{2,1,0:T(8,128)} %copy-done.1) | copy-start | bytes 5308420 | tf_op jit(solution)/shard_map/while
  103.0 11.5 %copy-start.1 = (f32[4,192,576]{2,1,0:T(8,128)}, f32[4,192,576]{2,1,0:T(8,128)S(1)}, u32[]{:S(2)}) copy-start(f32[4,192,576]{2,1,0:T(8,128)S(1)} %get-tuple-element.426) | copy-start | bytes 5308420 | tf_op jit(solution)/shard_map/while
  152.3 7.8 %copy-start.3 = (f32[512,512]{0,1:T(8,128)S(1)}, f32[512,512]{0,1:T(8,128)}, u32[]{:S(2)}) copy-start(f32[512,512]{0,1:T(8,128)} %get-tuple-element.410) | copy-start | bytes 3145732 | tf_op jit(solution)/shard_map/while
  152.3 7.8 %copy-start.5 = (f32[512,4,128]{0,2,1:T(8,128)S(1)}, f32[512,4,128]{0,2,1:T(8,128)}, u32[]{:S(2)}) copy-start(f32[512,4,128]{0,2,1:T(8,128)} %get-tuple-element.380) | copy-start | bytes 3145732 | tf_op jit(solution)/shard_map/while
  152.3 9.0 %copy-start.2 = (f32[4,192,576]{2,1,0:T(8,128)S(1)}, f32[4,192,576]{2,1,0:T(8,128)}, u32[]{:S(2)}) copy-start(f32[4,192,576]{2,1,0:T(8,128)} %copy-done.1) | copy-start | bytes 5308420 | tf_op jit(solution)/shard_map/while
  161.7 4.8 copy-start.11
  177.2 8.3 %copy-start = (f32[24,512,512]{2,1,0:T(8,128)}, f32[24,512,512]{2,1,0:T(8,128)S(1)}, u32[]{:S(2)}) copy-start(f32[24,512,512]{2,1,0:T(8,128)S(1)} %multiply_multiply_fusion.1) | copy-start | bytes 75497472
  185.9 22.2 %collective-permute-start.4 = (f32[24,32,512]{2,1,0:T(8,128)S(1)}, f32[24,32,512]{2,1,0:T(8,128)S(1)}, u32[]{:S(2)}, u32[]{:S(2)}) collective-permute-start(f32[24,32,512]{2,1,0:T(8,128)S(1)} %get-tuple-element.269), channel_id=1, source_target_pairs={{0,4},{4,8},{8,12},{12,16},{16,20},{20,24},{24,28},{1,5},{5,9},{9,... | collective-permute-start | bytes 4718600 | tf_op jit(solution)/shard_map/ppermute | solution.py:15
  190.7 22.6 %collective-permute-start.5 = (f32[24,32,512]{2,1,0:T(8,128)S(1)}, f32[24,32,512]{2,1,0:T(8,128)S(1)}, u32[]{:S(2)}, u32[]{:S(2)}) collective-permute-start(f32[24,32,512]{2,1,0:T(8,128)S(1)} %get-tuple-element.270), channel_id=1, source_target_pairs={{4,0},{8,4},{12,8},{16,12},{20,16},{24,20},{28,24},{5,1},{9,5},{13... | collective-permute-start | bytes 4718600 | tf_op jit(solution)/shard_map/ppermute | solution.py:18
  229.1 114.0 %collective-permute-start.6 = (f32[24,576,32]{1,2,0:T(8,128)}, f32[24,576,32]{1,2,0:T(8,128)}, u32[]{:S(2)}, u32[]{:S(2)}) collective-permute-start(f32[24,576,32]{1,2,0:T(8,128)} %copy.53), channel_id=1, source_target_pairs={{0,1},{1,2},{2,3},{4,5},{5,6},{6,7},{8,9},{9,10},{10,11},{12,13},{... | collective-permute-start | bytes 5308424 | tf_op jit(solution)/shard_map/ppermute | solution.py:15
  304.1 7.6 %copy-start.9 = (f32[24,65]{1,0:T(8,128)S(1)}, f32[24,65]{1,0:T(8,128)}, u32[]{:S(2)}) copy-start(f32[24,65]{1,0:T(8,128)} %param.12) | copy-start | bytes 18724
  304.1 7.7 %copy-start.10 = (f32[24,65]{1,0:T(8,128)S(1)}, f32[24,65]{1,0:T(8,128)}, u32[]{:S(2)}) copy-start(f32[24,65]{1,0:T(8,128)} %param.11) | copy-start | bytes 18724
  304.1 7.7 %copy-start.7 = (s32[128,192]{0,1:T(8,128)S(1)}, s32[128,192]{0,1:T(8,128)}, u32[]{:S(2)}) copy-start(s32[128,192]{0,1:T(8,128)} %copy-done.6) | copy-start | bytes 294916
  310.2 44.4 %collective-permute-start.7 = (f32[24,576,32]{1,2,0:T(8,128)}, f32[24,576,32]{1,2,0:T(8,128)}, u32[]{:S(2)}, u32[]{:S(2)}) collective-permute-start(f32[24,576,32]{1,2,0:T(8,128)} %copy.54), channel_id=1, source_target_pairs={{1,0},{2,1},{3,2},{5,4},{6,5},{7,6},{9,8},{10,9},{11,10},{13,12},{... | collective-permute-start | bytes 5308424 | tf_op jit(solution)/shard_map/ppermute | solution.py:18
  (2 other events, 1.9 us)
where the time goes:
time: 633 us; the launch traced here: 624 us
  local copies, waits for them, and re-layouts  203 us (32%)
  matrix products  200 us (32%)
  starting transfers between devices  93.3 us (15%)
  other arithmetic  67.8 us (11%)
  waiting for transfers between devices  57.2 us (9%)
    dot_general x3, matrix products, correlate(): jnp.einsum('gij,gbjc->gbic', row_table, stacked, precision=lax.Precision....  107 us
    ppermute x4, starting transfers between devices, padded(): lax.ppermute(lax.slice_in_dim(block, block.shape[dim] - width, None, axis...  86.7 us
    dot_general x5, matrix products, correlate(): jnp.einsum('gcrj,gij->grci', col_blocks, col_table, precision=lax.Precisi...  59.7 us
    another operation x5, local copies, waits for them, and re-layouts, correlate(): jnp.stack([row_pass[:, :, number * col_len:number * col_len + col_len + 2...  45.2 us
    ppermute x4, waiting for transfers between devices, padded(): lax.ppermute(lax.slice_in_dim(block, block.shape[dim] - width, None, axis...  42 us
    another operation x4, local copies, waits for them, and re-layouts, stack_rows(): jnp.stack([lax.slice_in_dim(extended, number * block_len, number * block_...  34.3 us
    dynamic_update_slice x4, local copies, waits for them, and re-layouts, forward_step(): fields = lax.dynamic_update_slice_in_dim(fields, field, first, 0)  33.9 us
    concatenate x2, other arithmetic, padded(): block = jnp.concatenate([low, block, high], axis=dim)  33.6 us
  transfers between devices with their start and end apart: 8, of which 6 were waited for; matrix products, arithmetic and copies ran while one was open for 5% of the time, Pallas kernels for 0%

commit v1 on v0

v1 whole, which is shorter than its diff:
```python
import functools

import jax
import jax.numpy as jnp
from jax import lax
from jax.experimental import pallas as pl
from jax.experimental.pallas import tpu as pltpu
from jax.sharding import PartitionSpec as P

resist_slope = 6.0
resist_level = 0.33
f32, bf16 = jnp.float32, jnp.bfloat16

FB = 16
AB = 32
CHUNK = 128
WIN = 256


def split(x):
    hi = x.astype(bf16)
    return hi, (x - hi.astype(f32)).astype(bf16)


def split_outside(x):
    hi = lax.reduce_precision(x, 8, 7)
    return hi.astype(bf16), (x - hi).astype(bf16)


def mm(a, b):
    return lax.dot_general(a, b, (((1,), (0,)), ((), ())), preferred_element_type=f32)


def tile_kernel(nk, height, breadth, reach, scal_ref, mask_ref, target_ref, fwd_ref, adj_ref, cvec_ref, avec_ref,
                resist_ref, grad_ref,
                mhi, mlo, ahi, alo, field, bhi, blo, z, chi, clo, dhi, dlo, inten):
    out_win = WIN - 2 * reach
    nwin = -(-breadth // out_win)
    span = FB + 2 * reach
    aspan = AB + 2 * reach
    rows3 = nwin * CHUNK

    inv_sum = scal_ref[0]
    for w in range(nwin):
        m = mask_ref[:, w * out_win:w * out_win + WIN]
        hi, lo = split(m)
        mhi[w] = hi
        mlo[w] = lo
    z[...] = jnp.zeros_like(z)

    def tables(k, carry):
        row = jnp.broadcast_to(cvec_ref[pl.ds(k, 1), :], (WIN, WIN))
        hi, lo = split(pltpu.roll(row, 0, 1, stride=1, stride_axis=0))
        chi[k] = hi
        clo[k] = lo
        row = jnp.broadcast_to(avec_ref[pl.ds(k, 1), :], (WIN, WIN))
        hi, lo = split(pltpu.roll(row, 0, 1, stride=1, stride_axis=0))
        dhi[k] = hi
        dlo[k] = lo
        return carry

    lax.fori_loop(0, nk, tables, 0)

    lane = lax.broadcasted_iota(jnp.int32, (CHUNK, WIN), 1)

    def chunk(c, carry):
        base = pl.multiple_of(c * CHUNK, CHUNK)

        def rows_forward(b, carry):
            start = pl.multiple_of(base + b * FB, FB)
            to = pl.multiple_of(b * FB, FB)
            for w in range(nwin):
                xh = mhi[w, pl.ds(start, span), :]
                xl = mlo[w, pl.ds(start, span), :]
                x = jnp.concatenate([xh, xl, xh, jnp.zeros((256 - 3 * span, WIN), bf16)], axis=0)
                y = mm(fwd_ref[...], x)
                hi, lo = split(y)
                ahi[:, pl.ds(w * CHUNK + to, FB), :] = hi.reshape(nk, FB, WIN)
                alo[:, pl.ds(w * CHUNK + to, FB), :] = lo.reshape(nk, FB, WIN)
            return carry

        lax.fori_loop(0, CHUNK // FB, rows_forward, 0)
        inten[...] = jnp.zeros_like(inten)

        def cols_forward(k, carry):
            ah, al = ahi[k], alo[k]
            ch, cl = chi[k], clo[k]
            f = mm(jnp.concatenate([ah, al, ah], axis=1), jnp.concatenate([ch, ch, cl], axis=0))
            field[k] = f
            inten[...] += f * f
            return carry

        lax.fori_loop(0, nk, cols_forward, 0)

        t = target_ref[pl.ds(base, CHUNK), :]
        outs = []
        for w in range(nwin):
            width = min(out_win, breadth - w * out_win)
            tw = t[:, w * out_win:min(w * out_win + WIN, breadth)]
            if tw.shape[1] < WIN:
                tw = jnp.concatenate([tw, jnp.zeros((CHUNK, WIN - tw.shape[1]), f32)], axis=1)
            i = inten[w * CHUNK:(w + 1) * CHUNK, :] * inv_sum
            r = 1.0 / (1.0 + jnp.exp(-resist_slope * (i - resist_level)))
            e = (r - tw) * resist_slope * r * (1.0 - r) * (2.0 * inv_sum)
            inten[w * CHUNK:(w + 1) * CHUNK, :] = jnp.where(lane < width, e, 0.0)
            outs.append(r[:, :width])
        resist_ref[pl.ds(base, CHUNK), :] = jnp.concatenate(outs, axis=1)

        def cols_adjoint(k, carry):
            gh, gl = split(field[k] * inten[...])
            dh, dl = dhi[k], dlo[k]
            b = mm(jnp.concatenate([gh, gl, gh], axis=1), jnp.concatenate([dh, dh, dl], axis=0))
            hi, lo = split(b)
            to = pl.multiple_of(k * AB, AB)
            bhi[:, pl.ds(to, AB), :] = hi.reshape(rows3 // AB, AB, WIN)
            blo[:, pl.ds(to, AB), :] = lo.reshape(rows3 // AB, AB, WIN)
            return carry

        lax.fori_loop(0, nk, cols_adjoint, 0)

        def rows_adjoint(b, carry):
            start = pl.multiple_of(base + b * AB, AB)
            for w in range(nwin):
                at = w * (CHUNK // AB) + b
                p = mm(adj_ref[...], bhi[at])
                q = mm(adj_ref[:aspan, :], blo[at])
                z[w, pl.ds(start, aspan), :] += p[:aspan] + p[aspan:] + q
            return carry

        lax.fori_loop(0, CHUNK // AB, rows_adjoint, 0)
        return carry

    lax.fori_loop(0, height // CHUNK, chunk, 0)

    both = 2 * reach
    pieces = []
    for w in range(nwin):
        left = z[w, :, :both]
        if w:
            left = left + z[w - 1, :, out_win:]
        pieces.append(left)
        end = min(out_win, breadth + both - w * out_win)
        pieces.append(z[w, :, both:end])
    grad_ref[...] = jnp.concatenate(pieces, axis=1)


def shift_pairs(axis):
    count = lax.axis_size(axis)
    forward = [(i, i + 1) for i in range(count - 1)]
    return forward, [(b, a) for a, b in forward]


def padded(block, sides, width):
    for axis, dim in sides:
        forward, backward = shift_pairs(axis)
        size = block.shape[dim]
        low = lax.ppermute(lax.slice_in_dim(block, size - width, size, axis=dim), axis, forward)
        high = lax.ppermute(lax.slice_in_dim(block, 0, width, axis=dim), axis, backward)
        block = jnp.concatenate([low, block, high], axis=dim)
    return block


def folded(block, sides, width):
    for axis, dim in sides:
        forward, backward = shift_pairs(axis)
        size = block.shape[dim]
        low = lax.ppermute(lax.slice_in_dim(block, size - width, size, axis=dim), axis, forward)
        high = lax.ppermute(lax.slice_in_dim(block, 0, width, axis=dim), axis, backward)
        inner = lax.slice_in_dim(block, width, size - width, axis=dim)
        rest = size - 3 * width
        lows = [(0, 0, 0), (0, 0, 0)]
        highs = [(0, 0, 0), (0, 0, 0)]
        lows[dim] = (0, rest, 0)
        highs[dim] = (rest, 0, 0)
        block = inner + lax.pad(low, 0.0, lows) + lax.pad(high, 0.0, highs)
    return block


def toeplitz(taps, block):
    span = taps.shape[1]
    length = block + span - 1
    p = jnp.arange(span)[:, None, None]
    i = jnp.arange(block)[None, :, None]
    j = jnp.arange(length)[None, None, :]
    onehot = (j - i == p).astype(bf16)
    return jnp.einsum("kp,pij->kij", taps, onehot, preferred_element_type=f32).astype(bf16)


def shards(mask, row_taps, col_taps, kernel_weights, target, density):
    height, breadth = mask.shape
    nk, taps = row_taps.shape
    reach = (taps - 1) // 2
    count = (nk // 3) * (density[0, 0] + 1)
    active = jnp.arange(nk) < count
    inv_sum = 1.0 / jnp.sum(jnp.where(active, kernel_weights, 0.0))
    scale = jnp.where(active, jnp.sqrt(kernel_weights), 0.0)

    out_win = WIN - 2 * reach
    nwin = -(-breadth // out_win)
    need = (nwin - 1) * out_win + WIN
    ext = padded(mask, (("row", 0), ("col", 1)), reach)
    ext = jnp.pad(ext, ((0, 0), (0, need - ext.shape[1])))

    rhi, rlo = split_outside(row_taps * scale[:, None])
    both = jnp.concatenate([rhi, rlo], axis=0)
    fwd = toeplitz(both, FB).reshape(2, nk * FB, FB + 2 * reach)
    fwd = jnp.concatenate([fwd[0], fwd[0], fwd[1], jnp.zeros((nk * FB, 256 - 3 * fwd.shape[2]), bf16)], axis=1)
    adj = toeplitz(both, AB).reshape(2, nk, AB, AB + 2 * reach)
    adj = adj.transpose(0, 3, 1, 2).reshape(2 * (AB + 2 * reach), nk * AB)
    avec = jnp.pad(col_taps, ((0, 0), (0, WIN - taps)))
    cvec = jnp.concatenate([col_taps[:, :1], jnp.zeros((nk, WIN - taps), f32), col_taps[:, :0:-1]], axis=1)

    eh = height + 2 * reach
    rows3 = nwin * CHUNK
    vmem = pl.BlockSpec(memory_space=pltpu.VMEM)
    resist, grad = pl.pallas_call(
        functools.partial(tile_kernel, nk, height, breadth, reach),
        out_shape=(
            jax.ShapeDtypeStruct((height, breadth), f32),
            jax.ShapeDtypeStruct((eh, breadth + 2 * reach), f32),
        ),
        in_specs=[pl.BlockSpec(memory_space=pltpu.SMEM)] + [vmem] * 6,
        out_specs=(vmem, vmem),
        scratch_shapes=[
            pltpu.VMEM((nwin, eh, WIN), bf16),
            pltpu.VMEM((nwin, eh, WIN), bf16),
            pltpu.VMEM((nk, rows3, WIN), bf16),
            pltpu.VMEM((nk, rows3, WIN), bf16),
            pltpu.VMEM((nk, rows3, WIN), f32),
            pltpu.VMEM((rows3 // AB, nk * AB, WIN), bf16),
            pltpu.VMEM((rows3 // AB, nk * AB, WIN), bf16),
            pltpu.VMEM((nwin, eh, WIN), f32),
        ] + [pltpu.VMEM((nk, WIN, WIN), bf16)] * 4 + [pltpu.VMEM((rows3, WIN), f32)],
        compiler_params=pltpu.CompilerParams(vmem_limit_bytes=60 * 1024 * 1024),
    )(inv_sum[None], ext, target, fwd, adj, cvec, avec)
    gradient = folded(grad, (("col", 1), ("row", 0)), reach)
    return resist, gradient


def solution(mesh):
    return jax.shard_map(
        shards,
        mesh=mesh,
        in_specs=(P("row", "col"), P(), P(), P(), P("row", "col"), P("row", "col")),
        out_specs=(P("row", "col"), P("row", "col")),
        check_vma=False,
    )
```

time: 633 us -> 148 us (0.23); the launches traced: 624 us -> 147 us
  matrix products: 200 us -> 0.6 us
  local copies, waits for them, and re-layouts: 203 us -> 4.86 us
  Pallas kernels: 0 us -> 91.3 us
  starting transfers between devices: 93.3 us -> 21.2 us
  other arithmetic: 67.8 us -> 8.09 us
  waiting for transfers between devices: 57.2 us -> 18.6 us
    dot_general x14 -> x2, matrix products: 200 us -> 0.6 us  [toeplitz(): jnp.einsum('kp,pij->kij', taps, onehot, preferred_element_type=f32)]
    pallas_call x0 -> x1, Pallas kernels: none -> 91.3 us  [shards(): pl.pallas_call(functools.partial(tile_kernel, nk, height, breadth, reach)...]
    another operation x10 -> x0, local copies, waits for them, and re-layouts: 80.6 us -> none  [the longest x5 45.2 us: correlate(): jnp.stack([row_pass[:, :, number * col_len:number * col_len + col_len + 2...]
    ppermute x4 -> x6, starting transfers between devices: 86.7 us -> 17.3 us  [the longest x2 7.1 us: padded(): lax.ppermute(lax.slice_in_dim(block, size - width, size, axis=dim), axis,...]
    dynamic_update_slice x4 -> x0, local copies, waits for them, and re-layouts: 33.9 us -> none  [forward_step(): fields = lax.dynamic_update_slice_in_dim(fields, field, first, 0)]
    concatenate x2 -> x1, other arithmetic: 33.6 us -> 1.64 us  [padded(): block = jnp.concatenate([low, block, high], axis=dim)]
    ppermute x4 -> x6, waiting for transfers between devices: 42 us -> 14.5 us  [the longest x2 8.36 us: folded(): lax.ppermute(lax.slice_in_dim(block, 0, width, axis=dim), axis, backward)]
    reshape x5 -> x3, local copies, waits for them, and re-layouts: 24.3 us -> 1.48 us  [the longest x2 1.08 us: shards(): adj = adj.transpose(0, 3, 1, 2).reshape(2 * (AB + 2 * reach), nk * AB)]
  transfers between devices with their start and end apart: 8 -> 8, of which waited for: 6 -> 5; matrix products, arithmetic and copies ran while one was open for 5% -> 5% of each run, Pallas kernels for 0% -> 0%
where the time goes in v1:
time: 148 us; the launch traced here: 147 us
  Pallas kernels  91.3 us (62%)
  starting transfers between devices  21.2 us (14%)
  waiting for transfers between devices  18.6 us (13%)
  other arithmetic  8.09 us (5%)
  local copies, waits for them, and re-layouts  4.86 us (3%)
  between operations  2.2 us (1%)
    pallas_call x1, Pallas kernels, shards(): pl.pallas_call(functools.partial(tile_kernel, nk, height, breadth, reach)...  91.3 us
    ppermute x2, waiting for transfers between devices, folded(): lax.ppermute(lax.slice_in_dim(block, 0, width, axis=dim), axis, backward)  8.36 us
    ppermute x2, starting transfers between devices, padded(): lax.ppermute(lax.slice_in_dim(block, size - width, size, axis=dim), axis,...  7.1 us
    ppermute x2, starting transfers between devices, folded(): lax.ppermute(lax.slice_in_dim(block, size - width, size, axis=dim), axis,...  7.03 us
    ppermute x2, waiting for transfers between devices, folded(): lax.ppermute(lax.slice_in_dim(block, size - width, size, axis=dim), axis,...  5.1 us
    ppermute x2, waiting for transfers between devices, padded(): lax.ppermute(lax.slice_in_dim(block, 0, width, axis=dim), axis, backward)  4.12 us
    ppermute x2, starting transfers between devices, padded(): lax.ppermute(lax.slice_in_dim(block, 0, width, axis=dim), axis, backward)  3.88 us
    ppermute x2, starting transfers between devices, folded(): lax.ppermute(lax.slice_in_dim(block, 0, width, axis=dim), axis, backward)  3.21 us
  transfers between devices with their start and end apart: 8, of which 5 were waited for; matrix products, arithmetic and copies ran while one was open for 5% of the time, Pallas kernels for 0%

profile of v1, /device:TPU:3, one launch (start us, length us, event | category | flops | bytes accessed | tf_op | source)
XLA Modules:
  0.0 146.9 jit_solution(12288036332902165149)
XLA Ops:
  0.6 1.0 fusion.10
  1.6 2.6 %collective-permute-start.1 = (f32[32,512]{1,0:T(8,128)S(1)}, f32[32,512]{1,0:T(8,128)S(1)}, u32[]{:S(2)}, u32[]{:S(2)}) collective-permute-start(f32[32,512]{1,0:T(8,128)S(1)} %get-tuple-element.12), channel_id=1, source_target_pairs={{4,0},{8,4},{12,8},{16,12},{20,16},{24,20},{28,24},{5,1},{9,5},{13... | collective-permute-start | bytes 196616 | tf_op jit(solution)/shard_map/ppermute | solution.py:158
  4.2 3.9 %collective-permute-start = (f32[32,512]{1,0:T(8,128)S(1)}, f32[32,512]{1,0:T(8,128)S(1)}, u32[]{:S(2)}, u32[]{:S(2)}) collective-permute-start(f32[32,512]{1,0:T(8,128)S(1)} %get-tuple-element.13), channel_id=1, source_target_pairs={{0,4},{4,8},{8,12},{12,16},{16,20},{20,24},{24,28},{1,5},{5,9},{9,... | collective-permute-start | bytes 196616 | tf_op jit(solution)/shard_map/ppermute | solution.py:157
  8.8 1.3 compare_select_fusion
  10.0 0.8 reduce-precision_convert_fusion
  11.6 0.8 maximum_maximum_fusion.fwd_ref
  12.9 3.2 %collective-permute-start.2 = (f32[576,32]{1,0:T(8,128)S(1)}, f32[576,32]{1,0:T(8,128)S(1)}, u32[]{:S(2)}, u32[]{:S(2)}) collective-permute-start(f32[576,32]{1,0:T(8,128)S(1)} %get-tuple-element.10), channel_id=1, source_target_pairs={{0,1},{1,2},{2,3},{4,5},{5,6},{6,7},{8,9},{9,10},{10,11},{12,13},{... | collective-permute-start | bytes 221192 | tf_op jit(solution)/shard_map/ppermute | solution.py:157
  16.2 1.3 collective-permute-start.3
  17.5 0.7 pad_maximum_fusion.cvec_ref
  19.4 0.9 copy.14.adj_ref
  20.9 1.0 collective-permute-done.2
  22.0 4.1 %collective-permute-done.3 = f32[576,32]{1,0:T(8,128)S(1)} collective-permute-done((f32[576,32]{1,0:T(8,128)S(1)}, f32[576,32]{1,0:T(8,128)S(1)}, u32[]{:S(2)}, u32[]{:S(2)}) %collective-permute-start.3) | collective-permute-done | bytes 73760 | tf_op jit(solution)/shard_map/ppermute | solution.py:158
  26.1 1.6 %select_maximum_fusion.mask_ref = f32[576,640]{1,0:T(8,128)} fusion(f32[576,32]{1,0:T(8,128)S(1)} %collective-permute-done.3, f32[576,512]{1,0:T(8,128)S(1)} %constant_dynamic-update-slice_fusion, f32[576,32]{1,0:T(8,128)S(1)} %collective-permute-done.2), kind=kLoop, calls=%fused_computation | loop fusion | flops 2211840 | bytes 2801664 | tf_op jit(solution)/shard_map/concatenate | solution.py:159
  27.7 91.3 %shard_map.77 = (f32[512,512]{1,0:T(8,128)}, f32[576,576]{1,0:T(8,128)}) custom-call(f32[1]{0:T(128)} %bitcast.1.scal_ref, f32[576,640]{1,0:T(8,128)} %select_maximum_fusion.mask_ref, f32[512,512]{1,0:T(8,128)} %target_ref.1, bf16[384,256]{1,0:T(8,128)(2,1)} %maximum_maximum_fusion.fwd_ref, bf16[192,768]{1,0:T(8,128)(2,1)} %copy.14.adj_ref, ...), custom_call_target="tpu_custom_call" | custom-call | tf_op jit(solution)/shard_map/pallas_call | solution.py:216
  119.0 1.2 fusion.7
  120.2 3.2 %collective-permute-start.4 = (f32[576,32]{1,0:T(8,128)S(1)}, f32[576,32]{1,0:T(8,128)S(1)}, u32[]{:S(2)}, u32[]{:S(2)}) collective-permute-start(f32[576,32]{1,0:T(8,128)S(1)} %get-tuple-element.6), channel_id=1, source_target_pairs={{0,1},{1,2},{2,3},{4,5},{5,6},{6,7},{8,9},{9,10},{10,11},{12,13},{... | collective-permute-start | bytes 221192 | tf_op jit(solution)/shard_map/ppermute | solution.py:167
  123.5 1.3 collective-permute-start.5
  124.8 5.1 %collective-permute-done.4 = f32[576,32]{1,0:T(8,128)S(1)} collective-permute-done((f32[576,32]{1,0:T(8,128)S(1)}, f32[576,32]{1,0:T(8,128)S(1)}, u32[]{:S(2)}, u32[]{:S(2)}) %collective-permute-start.4) | collective-permute-done | bytes 73760 | tf_op jit(solution)/shard_map/ppermute | solution.py:167
  129.9 3.8 %collective-permute-done.5 = f32[576,32]{1,0:T(8,128)S(1)} collective-permute-done((f32[576,32]{1,0:T(8,128)S(1)}, f32[576,32]{1,0:T(8,128)S(1)}, u32[]{:S(2)}, u32[]{:S(2)}) %collective-permute-start.5) | collective-permute-done | bytes 73760 | tf_op jit(solution)/shard_map/ppermute | solution.py:168
  133.7 1.8 %pad_add_fusion = f32[576,512]{1,0:T(8,128)S(1)} fusion(f32[576,32]{1,0:T(8,128)S(1)} %collective-permute-done.5, f32[576,32]{1,0:T(8,128)S(1)} %collective-permute-done.4, f32[576,576]{1,0:T(8,128)} %get-tuple-element.5), kind=kLoop, calls=%fused_computation.4 | loop fusion | flops 589824 | bytes 2506752 | tf_op jit(solution)/shard_map/add | solution.py:175
  135.5 3.8 %collective-permute-start.6 = (f32[32,512]{1,0:T(8,128)S(1)}, f32[32,512]{1,0:T(8,128)S(1)}, u32[]{:S(2)}, u32[]{:S(2)}) collective-permute-start(f32[32,512]{1,0:T(8,128)S(1)} %get-tuple-element.8), channel_id=1, source_target_pairs={{0,4},{4,8},{8,12},{12,16},{16,20},{20,24},{24,28},{1,5},{5,9},{9,... | collective-permute-start | bytes 196616 | tf_op jit(solution)/shard_map/ppermute | solution.py:167
  139.3 1.9 %collective-permute-start.7 = (f32[32,512]{1,0:T(8,128)S(1)}, f32[32,512]{1,0:T(8,128)S(1)}, u32[]{:S(2)}, u32[]{:S(2)}) collective-permute-start(f32[32,512]{1,0:T(8,128)S(1)} %get-tuple-element.9), channel_id=1, source_target_pairs={{4,0},{8,4},{12,8},{16,12},{20,16},{24,20},{28,24},{5,1},{9,5},{13... | collective-permute-start | bytes 196616 | tf_op jit(solution)/shard_map/ppermute | solution.py:168
  141.3 4.5 %collective-permute-done.7 = f32[32,512]{1,0:T(8,128)S(1)} collective-permute-done((f32[32,512]{1,0:T(8,128)S(1)}, f32[32,512]{1,0:T(8,128)S(1)}, u32[]{:S(2)}, u32[]{:S(2)}) %collective-permute-start.7) | collective-permute-done | bytes 65568 | tf_op jit(solution)/shard_map/ppermute | solution.py:168
  145.8 1.1 fusion
  (28 shorter events, 2.4 us)
Async XLA Ops:
  0.6 12.0 %copy-start = (f32[512,512]{1,0:T(8,128)S(1)}, f32[512,512]{1,0:T(8,128)}, u32[]{:S(2)}) copy-start(f32[512,512]{1,0:T(8,128)} %param.6) | copy-start | bytes 3145732
  0.6 11.8 %copy-start.1 = (f32[24,65]{1,0:T(8,128)S(1)}, f32[24,65]{1,0:T(8,128)}, u32[]{:S(2)}) copy-start(f32[24,65]{1,0:T(8,128)} %param.8) | copy-start | bytes 18724
  1.6 11.1 %collective-permute-start.1 = (f32[32,512]{1,0:T(8,128)S(1)}, f32[32,512]{1,0:T(8,128)S(1)}, u32[]{:S(2)}, u32[]{:S(2)}) collective-permute-start(f32[32,512]{1,0:T(8,128)S(1)} %get-tuple-element.12), channel_id=1, source_target_pairs={{4,0},{8,4},{12,8},{16,12},{20,16},{24,20},{28,24},{5,1},{9,5},{13... | collective-permute-start | bytes 196616 | tf_op jit(solution)/shard_map/ppermute | solution.py:158
  4.2 8.4 %collective-permute-start = (f32[32,512]{1,0:T(8,128)S(1)}, f32[32,512]{1,0:T(8,128)S(1)}, u32[]{:S(2)}, u32[]{:S(2)}) collective-permute-start(f32[32,512]{1,0:T(8,128)S(1)} %get-tuple-element.13), channel_id=1, source_target_pairs={{0,4},{4,8},{8,12},{12,16},{16,20},{20,24},{24,28},{1,5},{5,9},{9,... | collective-permute-start | bytes 196616 | tf_op jit(solution)/shard_map/ppermute | solution.py:157
  12.9 9.0 %collective-permute-start.2 = (f32[576,32]{1,0:T(8,128)S(1)}, f32[576,32]{1,0:T(8,128)S(1)}, u32[]{:S(2)}, u32[]{:S(2)}) collective-permute-start(f32[576,32]{1,0:T(8,128)S(1)} %get-tuple-element.10), channel_id=1, source_target_pairs={{0,1},{1,2},{2,3},{4,5},{5,6},{6,7},{8,9},{9,10},{10,11},{12,13},{... | collective-permute-start | bytes 221192 | tf_op jit(solution)/shard_map/ppermute | solution.py:157
  16.2 9.9 %collective-permute-start.3 = (f32[576,32]{1,0:T(8,128)S(1)}, f32[576,32]{1,0:T(8,128)S(1)}, u32[]{:S(2)}, u32[]{:S(2)}) collective-permute-start(f32[576,32]{1,0:T(8,128)S(1)} %get-tuple-element.11), channel_id=1, source_target_pairs={{1,0},{2,1},{3,2},{5,4},{6,5},{7,6},{9,8},{10,9},{11,10},{13,12},{... | collective-permute-start | bytes 221192 | tf_op jit(solution)/shard_map/ppermute | solution.py:158
  120.2 9.6 %collective-permute-start.4 = (f32[576,32]{1,0:T(8,128)S(1)}, f32[576,32]{1,0:T(8,128)S(1)}, u32[]{:S(2)}, u32[]{:S(2)}) collective-permute-start(f32[576,32]{1,0:T(8,128)S(1)} %get-tuple-element.6), channel_id=1, source_target_pairs={{0,1},{1,2},{2,3},{4,5},{5,6},{6,7},{8,9},{9,10},{10,11},{12,13},{... | collective-permute-start | bytes 221192 | tf_op jit(solution)/shard_map/ppermute | solution.py:167
  123.5 10.2 %collective-permute-start.5 = (f32[576,32]{1,0:T(8,128)S(1)}, f32[576,32]{1,0:T(8,128)S(1)}, u32[]{:S(2)}, u32[]{:S(2)}) collective-permute-start(f32[576,32]{1,0:T(8,128)S(1)} %get-tuple-element.7), channel_id=1, source_target_pairs={{1,0},{2,1},{3,2},{5,4},{6,5},{7,6},{9,8},{10,9},{11,10},{13,12},{... | collective-permute-start | bytes 221192 | tf_op jit(solution)/shard_map/ppermute | solution.py:168
  135.5 5.8 %collective-permute-start.6 = (f32[32,512]{1,0:T(8,128)S(1)}, f32[32,512]{1,0:T(8,128)S(1)}, u32[]{:S(2)}, u32[]{:S(2)}) collective-permute-start(f32[32,512]{1,0:T(8,128)S(1)} %get-tuple-element.8), channel_id=1, source_target_pairs={{0,4},{4,8},{8,12},{12,16},{16,20},{20,24},{24,28},{1,5},{5,9},{9,... | collective-permute-start | bytes 196616 | tf_op jit(solution)/shard_map/ppermute | solution.py:167
  139.3 6.5 %collective-permute-start.7 = (f32[32,512]{1,0:T(8,128)S(1)}, f32[32,512]{1,0:T(8,128)S(1)}, u32[]{:S(2)}, u32[]{:S(2)}) collective-permute-start(f32[32,512]{1,0:T(8,128)S(1)} %get-tuple-element.9), channel_id=1, source_target_pairs={{4,0},{8,4},{12,8},{16,12},{20,16},{24,20},{28,24},{5,1},{9,5},{13... | collective-permute-start | bytes 196616 | tf_op jit(solution)/shard_map/ppermute | solution.py:168

commit v2 on v1

--- a/solution.py
+++ b/solution.py
@@ -144,36 +144,126 @@
     grad_ref[...] = jnp.concatenate(pieces, axis=1)
 
 
-def shift_pairs(axis):
-    count = lax.axis_size(axis)
-    forward = [(i, i + 1) for i in range(count - 1)]
-    return forward, [(b, a) for a, b in forward]
-
-
-def padded(block, sides, width):
-    for axis, dim in sides:
-        forward, backward = shift_pairs(axis)
-        size = block.shape[dim]
-        low = lax.ppermute(lax.slice_in_dim(block, size - width, size, axis=dim), axis, forward)
-        high = lax.ppermute(lax.slice_in_dim(block, 0, width, axis=dim), axis, backward)
-        block = jnp.concatenate([low, block, high], axis=dim)
-    return block
-
-
-def folded(block, sides, width):
-    for axis, dim in sides:
-        forward, backward = shift_pairs(axis)
-        size = block.shape[dim]
-        low = lax.ppermute(lax.slice_in_dim(block, size - width, size, axis=dim), axis, forward)
-        high = lax.ppermute(lax.slice_in_dim(block, 0, width, axis=dim), axis, backward)
-        inner = lax.slice_in_dim(block, width, size - width, axis=dim)
-        rest = size - 3 * width
-        lows = [(0, 0, 0), (0, 0, 0)]
-        highs = [(0, 0, 0), (0, 0, 0)]
-        lows[dim] = (0, rest, 0)
-        highs[dim] = (rest, 0, 0)
-        block = inner + lax.pad(low, 0.0, lows) + lax.pad(high, 0.0, highs)
-    return block
+def sides(axis):
+    me, count = lax.axis_index(axis), lax.axis_size(axis)
+    return ((axis, me - 1, me > 0), (axis, me + 1, me < count - 1))
+
+
+def greet(neighbours):
+    barrier = pltpu.get_barrier_semaphore()
+    for axis, at, there in neighbours:
+        @pl.when(there)
+        def _():
+            pl.semaphore_signal(barrier, inc=1, device_id={axis: at}, device_id_type=pl.DeviceIdType.MESH)
+    pl.semaphore_wait(barrier, sum(there.astype(jnp.int32) for _, _, there in neighbours))
+
+
+def exchange(neighbours, sources, landing, send_sem, recv_sem):
+    def copy(i):
+        axis, at, _ = neighbours[i]
+        return pltpu.make_async_remote_copy(
+            src_ref=sources[i], dst_ref=landing.at[1 - i], send_sem=send_sem.at[i], recv_sem=recv_sem.at[1 - i],
+            device_id={axis: at}, device_id_type=pl.DeviceIdType.MESH)
+
+    def incoming(i):
+        axis, at, _ = neighbours[i]
+        return pltpu.make_async_remote_copy(
+            src_ref=sources[i], dst_ref=landing.at[i], send_sem=send_sem.at[i], recv_sem=recv_sem.at[i],
+            device_id={axis: at}, device_id_type=pl.DeviceIdType.MESH)
+
+    for i in range(2):
+        @pl.when(neighbours[i][2])
+        def _():
+            copy(i).start()
+    for i in range(2):
+        @pl.when(neighbours[i][2])
+        def _():
+            incoming(i).wait_recv()
+
+        @pl.when(jnp.logical_not(neighbours[i][2]))
+        def _():
+            landing[i] = jnp.zeros(landing.shape[1:], f32)
+    for i in range(2):
+        @pl.when(neighbours[i][2])
+        def _():
+            copy(i).wait_send()
+
+
+def pack(strip):
+    width = strip.shape[1]
+    folds = 128 // width
+    part = strip.shape[0] // folds
+    return jnp.concatenate([strip[i * part:(i + 1) * part] for i in range(folds)], axis=1)
+
+
+def unpack(packed, width):
+    return jnp.concatenate([packed[:, i:i + width] for i in range(0, 128, width)], axis=0)
+
+
+def widen_kernel(reach, mask_ref, ext_ref, rows, colsend, cols, sems):
+    height, breadth = mask_ref.shape
+    up_down, left_right = sides("row"), sides("col")
+    greet(up_down + left_right)
+    exchange(up_down, (mask_ref.at[pl.ds(0, reach)], mask_ref.at[pl.ds(height - reach, reach)]), rows, sems.at[0], sems.at[1])
+    colsend[0] = pack(jnp.concatenate([rows[0, :, :reach], mask_ref[:, :reach], rows[1, :, :reach]], axis=0))
+    colsend[1] = pack(jnp.concatenate(
+        [rows[0, :, breadth - reach:], mask_ref[:, breadth - reach:], rows[1, :, breadth - reach:]], axis=0))
+    exchange(left_right, (colsend.at[0], colsend.at[1]), cols, sems.at[2], sems.at[3])
+    left, right = unpack(cols[0], reach), unpack(cols[1], reach)
+    extra = ext_ref.shape[1] - breadth - 2 * reach
+    for part, lo, hi in ((rows[0], 0, reach), (mask_ref[...], reach, reach + height),
+                         (rows[1], reach + height, height + 2 * reach)):
+        ext_ref[lo:hi, :] = jnp.concatenate(
+            [left[lo:hi], part, right[lo:hi], jnp.zeros((hi - lo, extra), f32)], axis=1)
+
+
+def fold_kernel(reach, g_ref, out_ref, colsend, cols, acc, rows, sems):
+    height, breadth = out_ref.shape
+    up_down, left_right = sides("row"), sides("col")
+    greet(up_down + left_right)
+    colsend[0] = pack(g_ref[:, :reach])
+    colsend[1] = pack(g_ref[:, reach + breadth:])
+    exchange(left_right, (colsend.at[0], colsend.at[1]), cols, sems.at[0], sems.at[1])
+    left, right = unpack(cols[0], reach), unpack(cols[1], reach)
+    acc[...] = jnp.concatenate(
+        [g_ref[:, reach:2 * reach] + left, g_ref[:, 2 * reach:breadth], g_ref[:, breadth:breadth + reach] + right], axis=1)
+    exchange(up_down, (acc.at[pl.ds(0, reach)], acc.at[pl.ds(height + reach, reach)]), rows, sems.at[2], sems.at[3])
+    out_ref[:reach, :] = acc[reach:2 * reach, :] + rows[0]
+    out_ref[reach:height - reach, :] = acc[2 * reach:height, :]
+    out_ref[height - reach:, :] = acc[height:height + reach, :] + rows[1]
+
+
+def strips(height, breadth, reach):
+    packed = pltpu.VMEM((2, (height + 2 * reach) * reach // 128, 128), f32)
+    return packed, pltpu.VMEM((2, reach, breadth), f32), pltpu.SemaphoreType.DMA((4, 2))
+
+
+def widen(mask, reach, need):
+    height, breadth = mask.shape
+    packed, rows, sems = strips(height, breadth, reach)
+    vmem = pl.BlockSpec(memory_space=pltpu.VMEM)
+    return pl.pallas_call(
+        functools.partial(widen_kernel, reach),
+        out_shape=jax.ShapeDtypeStruct((height + 2 * reach, need), f32),
+        in_specs=[vmem], out_specs=vmem,
+        scratch_shapes=[rows, packed, packed, sems],
+        compiler_params=pltpu.CompilerParams(
+            collective_id=0, has_side_effects=True, vmem_limit_bytes=16 * 1024 * 1024),
+    )(mask)
+
+
+def fold(grad, reach):
+    height, breadth = grad.shape[0] - 2 * reach, grad.shape[1] - 2 * reach
+    packed, rows, sems = strips(height, breadth, reach)
+    vmem = pl.BlockSpec(memory_space=pltpu.VMEM)
+    return pl.pallas_call(
+        functools.partial(fold_kernel, reach),
+        out_shape=jax.ShapeDtypeStruct((height, breadth), f32),
+        in_specs=[vmem], out_specs=vmem,
+        scratch_shapes=[packed, packed, pltpu.VMEM((height + 2 * reach, breadth), f32), rows, sems],
+        compiler_params=pltpu.CompilerParams(
+            collective_id=1, has_side_effects=True, vmem_limit_bytes=16 * 1024 * 1024),
+    )(grad)
 
 
 def toeplitz(taps, block):
@@ -198,8 +288,7 @@
     out_win = WIN - 2 * reach
     nwin = -(-breadth // out_win)
     need = (nwin - 1) * out_win + WIN
-    ext = padded(mask, (("row", 0), ("col", 1)), reach)
-    ext = jnp.pad(ext, ((0, 0), (0, need - ext.shape[1])))
+    ext = widen(mask, reach, need)
 
     rhi, rlo = split_outside(row_taps * scale[:, None])
     both = jnp.concatenate([rhi, rlo], axis=0)
@@ -233,7 +322,7 @@
         ] + [pltpu.VMEM((nk, WIN, WIN), bf16)] * 4 + [pltpu.VMEM((rows3, WIN), f32)],
         compiler_params=pltpu.CompilerParams(vmem_limit_bytes=60 * 1024 * 1024),
     )(inv_sum[None], ext, target, fwd, adj, cvec, avec)
-    gradient = folded(grad, (("col", 1), ("row", 0)), reach)
+    gradient = fold(grad, reach)
     return resist, gradient
 
 

time: 148 us -> 126 us (0.85)
  starting transfers between devices: 21.2 us -> 0 us
  Pallas kernels: 91.3 us -> 111 us
  waiting for transfers between devices: 18.6 us -> 0 us
  other arithmetic: 8.09 us -> 4.3 us
  local copies, waits for them, and re-layouts: 4.86 us -> 7.33 us
    ppermute x8 -> x0, starting transfers between devices: 21.2 us -> none  [the longest x2 7.1 us: padded(): lax.ppermute(lax.slice_in_dim(block, size - width, size, axis=dim), axis,...]
    pallas_call x0 -> x2, Pallas kernels: none -> 19.7 us  [the longest x1 10.6 us: fold(): pl.pallas_call(functools.partial(fold_kernel, reach), out_shape=jax.Shape...]
    ppermute x8 -> x0, waiting for transfers between devices: 18.6 us -> none  [the longest x2 8.36 us: folded(): lax.ppermute(lax.slice_in_dim(block, 0, width, axis=dim), axis, backward)]
    unnamed x6 -> x7, local copies, waits for them, and re-layouts: 0.08 us -> 3.47 us
    add x2 -> x0, other arithmetic: 2.89 us -> none  [folded(): block = inner + lax.pad(low, 0.0, lows) + lax.pad(high, 0.0, highs)]
    slice x4 -> x0, local copies, waits for them, and re-layouts: 2.33 us -> none  [the longest x2 1.21 us: folded(): lax.slice_in_dim(block, size - width, size, axis=dim)]
    concatenate x1 -> x0, other arithmetic: 1.64 us -> none  [padded(): block = jnp.concatenate([low, block, high], axis=dim)]
  transfers between devices with their start and end apart: 8 -> 0, of which waited for: 5 -> 0; matrix products, arithmetic and copies ran while one was open for 5% -> 0% of each run, Pallas kernels for 0% -> 0%
where the time goes in v2:
time: 126 us; the launch traced here: 125 us
  Pallas kernels  111 us (88%)
  local copies, waits for them, and re-layouts  7.33 us (6%)
  other arithmetic  4.3 us (3%)
  between operations  2.08 us (2%)
    pallas_call x1, Pallas kernels, shards(): pl.pallas_call(functools.partial(tile_kernel, nk, height, breadth, reach)...  91.3 us
    pallas_call x1, Pallas kernels, fold(): pl.pallas_call(functools.partial(fold_kernel, reach), out_shape=jax.Shape...  10.6 us
    pallas_call x1, Pallas kernels, widen(): pl.pallas_call(functools.partial(widen_kernel, reach), out_shape=jax.Shap...  9.16 us
    unnamed x7, local copies, waits for them, and re-layouts  3.47 us

profile of v2, /device:TPU:3, one launch (start us, length us, event | category | flops | bytes accessed | tf_op | source)
XLA Modules:
  0.0 125.3 jit_solution(11347797633270705536)
XLA Ops:
  1.3 0.1 pad.11.clone
  1.4 1.3 %compare_select_fusion = (f32[24]{0:T(128)S(1)}, f32[]{:T(128)}) fusion(f32[24]{0:T(128)} %param.9, s32[]{:T(128)} %bitcast), kind=kLoop, calls=%fused_computation.15 | loop fusion | flops 95 | bytes 200 | tf_op jit(solution)/shard_map/jit(_where)/select_n | solution.py:286
  3.3 0.1 pad.6.clone
  3.4 0.8 reduce-precision_convert_fusion
  4.2 0.8 slice.18
  5.0 0.1 rev.3
  5.0 1.4 %pad_maximum_fusion.cvec_ref = f32[24,256]{1,0:T(8,128)} fusion(f32[24,64]{1,0:T(8,128)S(1)} %rev.3, f32[24,1]{1,0:T(8,128)} %bitcast.19, f32[256]{0:T(256)S(1)} %pad.6.clone), kind=kLoop, calls=%fused_computation.8 | loop fusion | flops 12288 | bytes 31840 | tf_op jit(solution)/shard_map/concatenate | solution.py:300
  6.4 1.3 %pad.4.avec_ref = f32[24,256]{1,0:T(8,128)} pad(f32[24,65]{1,0:T(8,128)} %param.8, f32[]{:T(128)} %constant.4.clone.1), padding=0_0x0_191 | pad | bytes 30820 | tf_op jit(solution)/shard_map/jit(_pad)/pad | solution.py:299
  7.8 0.2 convolution_convert_fusion.1
  8.1 0.0 copy-start.2
  8.1 0.8 maximum_maximum_fusion.fwd_ref
  8.9 0.4 convolution_convert_fusion
  9.3 0.4 copy.16
  9.7 0.2 reshape.51
  9.9 0.9 copy.14.adj_ref
  10.8 0.0 copy-done.2
  10.8 9.2 %shard_map.77.mask_ref = f32[576,640]{1,0:T(8,128)S(1)} custom-call(f32[512,512]{1,0:T(8,128)S(1)} %copy-done.2), custom_call_target="tpu_custom_call" | custom-call | tf_op jit(solution)/shard_map/pallas_call | solution.py:245
  20.0 0.0 copy-start
  20.0 1.1 copy-done
  21.1 91.3 %shard_map.78 = (f32[512,512]{1,0:T(8,128)}, f32[576,576]{1,0:T(8,128)}) custom-call(f32[1]{0:T(128)} %bitcast.1.scal_ref, f32[576,640]{1,0:T(8,128)} %copy-done, f32[512,512]{1,0:T(8,128)} %target_ref.1, bf16[384,256]{1,0:T(8,128)(2,1)} %maximum_maximum_fusion.fwd_ref, bf16[192,768]{1,0:T(8,128)(2,1)} %copy.14.adj_ref, f32[24,256]{1,0:T(8,128)} %pad_maximum_fusion.cvec_ref, ...), custom_call_target="tpu_custom_call" | custom-call | tf_op jit(solution)/shard_map/pallas_call | solution.py:305
  112.4 0.0 copy-start.1
  112.4 1.4 %copy-done.1 = f32[576,576]{1,0:T(8,128)S(1)} copy-done((f32[576,576]{1,0:T(8,128)S(1)}, f32[576,576]{1,0:T(8,128)}, u32[]{:S(2)}) %copy-start.1) | copy-done | bytes 1327128
  113.8 10.6 %shard_map.79 = f32[512,512]{1,0:T(8,128)S(1)} custom-call(f32[576,576]{1,0:T(8,128)S(1)} %copy-done.1), custom_call_target="tpu_custom_call" | custom-call | tf_op jit(solution)/shard_map/pallas_call | solution.py:259
  124.4 1.0 copy.19
  (7 shorter events, 0.1 us)
Async XLA Ops:
  8.1 2.7 %copy-start.2 = (f32[512,512]{1,0:T(8,128)S(1)}, f32[512,512]{1,0:T(8,128)}, u32[]{:S(2)}) copy-start(f32[512,512]{1,0:T(8,128)} %mask_ref.1) | copy-start | bytes 3145732
  20.0 1.1 copy-start
  112.4 1.4 %copy-start.1 = (f32[576,576]{1,0:T(8,128)S(1)}, f32[576,576]{1,0:T(8,128)}, u32[]{:S(2)}) copy-start(f32[576,576]{1,0:T(8,128)} %get-tuple-element.5.g_ref) | copy-start | bytes 3981316

commit v3 on v2

--- a/solution.py
+++ b/solution.py
@@ -79,7 +79,7 @@
                 alo[:, pl.ds(w * CHUNK + to, FB), :] = lo.reshape(nk, FB, WIN)
             return carry
 
-        lax.fori_loop(0, CHUNK // FB, rows_forward, 0)
+        lax.fori_loop(0, CHUNK // FB, rows_forward, 0, unroll=4)
         inten[...] = jnp.zeros_like(inten)
 
         def cols_forward(k, carry):
@@ -90,7 +90,7 @@
             inten[...] += f * f
             return carry
 
-        lax.fori_loop(0, nk, cols_forward, 0)
+        lax.fori_loop(0, nk, cols_forward, 0, unroll=8)
 
         t = target_ref[pl.ds(base, CHUNK), :]
         outs = []
@@ -116,7 +116,7 @@
             blo[:, pl.ds(to, AB), :] = lo.reshape(rows3 // AB, AB, WIN)
             return carry
 
-        lax.fori_loop(0, nk, cols_adjoint, 0)
+        lax.fori_loop(0, nk, cols_adjoint, 0, unroll=8)
 
         def rows_adjoint(b, carry):
             start = pl.multiple_of(base + b * AB, AB)
@@ -127,7 +127,7 @@
                 z[w, pl.ds(start, aspan), :] += p[:aspan] + p[aspan:] + q
             return carry
 
-        lax.fori_loop(0, CHUNK // AB, rows_adjoint, 0)
+        lax.fori_loop(0, CHUNK // AB, rows_adjoint, 0, unroll=4)
         return carry
 
     lax.fori_loop(0, height // CHUNK, chunk, 0)

time: 126 us -> 96.6 us (0.77)
  Pallas kernels: 111 us -> 81.4 us
    pallas_call x1, Pallas kernels: 91.3 us -> 61.6 us  [shards(): pl.pallas_call(functools.partial(tile_kernel, nk, height, breadth, reach)...]
where the time goes in v3:
time: 96.6 us; the launch traced here: 95.7 us
  Pallas kernels  81.4 us (84%)
  local copies, waits for them, and re-layouts  7.33 us (8%)
  other arithmetic  4.3 us (4%)
  between operations  2.08 us (2%)
    pallas_call x1, Pallas kernels, shards(): pl.pallas_call(functools.partial(tile_kernel, nk, height, breadth, reach)...  61.6 us
    pallas_call x1, Pallas kernels, fold(): pl.pallas_call(functools.partial(fold_kernel, reach), out_shape=jax.Shape...  10.6 us
    pallas_call x1, Pallas kernels, widen(): pl.pallas_call(functools.partial(widen_kernel, reach), out_shape=jax.Shap...  9.16 us
    unnamed x7, local copies, waits for them, and re-layouts  3.47 us

profile of v3, /device:TPU:3, one launch (start us, length us, event | category | flops | bytes accessed | tf_op | source)
XLA Modules:
  0.0 95.7 jit_solution(9726044069341628006)
XLA Ops:
  1.3 0.1 pad.11.clone
  1.4 1.3 %compare_select_fusion = (f32[24]{0:T(128)S(1)}, f32[]{:T(128)}) fusion(f32[24]{0:T(128)} %param.9, s32[]{:T(128)} %bitcast), kind=kLoop, calls=%fused_computation.15 | loop fusion | flops 95 | bytes 200 | tf_op jit(solution)/shard_map/jit(_where)/select_n | solution.py:286
  3.3 0.1 pad.6.clone
  3.4 0.8 reduce-precision_convert_fusion
  4.2 0.8 slice.18
  5.0 0.1 rev.3
  5.0 1.4 %pad_maximum_fusion.cvec_ref = f32[24,256]{1,0:T(8,128)} fusion(f32[24,64]{1,0:T(8,128)S(1)} %rev.3, f32[24,1]{1,0:T(8,128)} %bitcast.19, f32[256]{0:T(256)S(1)} %pad.6.clone), kind=kLoop, calls=%fused_computation.8 | loop fusion | flops 12288 | bytes 31840 | tf_op jit(solution)/shard_map/concatenate | solution.py:300
  6.4 1.3 %pad.4.avec_ref = f32[24,256]{1,0:T(8,128)} pad(f32[24,65]{1,0:T(8,128)} %param.8, f32[]{:T(128)} %constant.4.clone.1), padding=0_0x0_191 | pad | bytes 30820 | tf_op jit(solution)/shard_map/jit(_pad)/pad | solution.py:299
  7.8 0.2 convolution_convert_fusion.1
  8.1 0.0 copy-start.2
  8.1 0.8 maximum_maximum_fusion.fwd_ref
  8.9 0.4 convolution_convert_fusion
  9.3 0.4 copy.16
  9.7 0.2 reshape.51
  9.9 0.9 copy.14.adj_ref
  10.8 0.0 copy-done.2
  10.8 9.2 %shard_map.77.mask_ref = f32[576,640]{1,0:T(8,128)S(1)} custom-call(f32[512,512]{1,0:T(8,128)S(1)} %copy-done.2), custom_call_target="tpu_custom_call" | custom-call | tf_op jit(solution)/shard_map/pallas_call | solution.py:245
  20.0 0.0 copy-start
  20.0 1.1 %copy-done = f32[576,640]{1,0:T(8,128)} copy-done((f32[576,640]{1,0:T(8,128)}, f32[576,640]{1,0:T(8,128)S(1)}, u32[]{:S(2)}) %copy-start) | copy-done | bytes 1474584
  21.1 61.6 %shard_map.78 = (f32[512,512]{1,0:T(8,128)}, f32[576,576]{1,0:T(8,128)}) custom-call(f32[1]{0:T(128)} %bitcast.1.scal_ref, f32[576,640]{1,0:T(8,128)} %copy-done, f32[512,512]{1,0:T(8,128)} %target_ref.1, bf16[384,256]{1,0:T(8,128)(2,1)} %maximum_maximum_fusion.fwd_ref, bf16[192,768]{1,0:T(8,128)(2,1)} %copy.14.adj_ref, f32[24,256]{1,0:T(8,128)} %pad_maximum_fusion.cvec_ref, ...), custom_call_target="tpu_custom_call" | custom-call | tf_op jit(solution)/shard_map/pallas_call | solution.py:305
  82.7 0.0 copy-start.1
  82.7 1.4 %copy-done.1 = f32[576,576]{1,0:T(8,128)S(1)} copy-done((f32[576,576]{1,0:T(8,128)S(1)}, f32[576,576]{1,0:T(8,128)}, u32[]{:S(2)}) %copy-start.1) | copy-done | bytes 1327128
  84.1 10.6 %shard_map.79 = f32[512,512]{1,0:T(8,128)S(1)} custom-call(f32[576,576]{1,0:T(8,128)S(1)} %copy-done.1), custom_call_target="tpu_custom_call" | custom-call | tf_op jit(solution)/shard_map/pallas_call | solution.py:259
  94.7 1.0 %copy.19 = f32[512,512]{1,0:T(8,128)} copy(f32[512,512]{1,0:T(8,128)S(1)} %shard_map.79) | data formatting | bytes 2097152
  (7 shorter events, 0.1 us)
Async XLA Ops:
  8.1 2.7 %copy-start.2 = (f32[512,512]{1,0:T(8,128)S(1)}, f32[512,512]{1,0:T(8,128)}, u32[]{:S(2)}) copy-start(f32[512,512]{1,0:T(8,128)} %mask_ref.1) | copy-start | bytes 3145732
  20.0 1.1 %copy-start = (f32[576,640]{1,0:T(8,128)}, f32[576,640]{1,0:T(8,128)S(1)}, u32[]{:S(2)}) copy-start(f32[576,640]{1,0:T(8,128)S(1)} %shard_map.77.mask_ref) | copy-start | bytes 4423684
  82.7 1.4 %copy-start.1 = (f32[576,576]{1,0:T(8,128)S(1)}, f32[576,576]{1,0:T(8,128)}, u32[]{:S(2)}) copy-start(f32[576,576]{1,0:T(8,128)} %get-tuple-element.5.g_ref) | copy-start | bytes 3981316

commit v4 on v3

--- a/solution.py
+++ b/solution.py
@@ -13,7 +13,7 @@
 
 FB = 16
 AB = 32
-CHUNK = 128
+CHUNK = 256
 WIN = 256
 
 
@@ -33,7 +33,7 @@
 
 def tile_kernel(nk, height, breadth, reach, scal_ref, mask_ref, target_ref, fwd_ref, adj_ref, cvec_ref, avec_ref,
                 resist_ref, grad_ref,
-                mhi, mlo, ahi, alo, field, bhi, blo, z, chi, clo, dhi, dlo, inten):
+                mhi, mlo, ahi, alo, field, z, chi, clo, dhi, dlo, inten):
     out_win = WIN - 2 * reach
     nwin = -(-breadth // out_win)
     span = FB + 2 * reach
@@ -90,7 +90,7 @@
             inten[...] += f * f
             return carry
 
-        lax.fori_loop(0, nk, cols_forward, 0, unroll=8)
+        lax.fori_loop(0, nk, cols_forward, 0, unroll=4)
 
         t = target_ref[pl.ds(base, CHUNK), :]
         outs = []
@@ -111,19 +111,18 @@
             dh, dl = dhi[k], dlo[k]
             b = mm(jnp.concatenate([gh, gl, gh], axis=1), jnp.concatenate([dh, dh, dl], axis=0))
             hi, lo = split(b)
-            to = pl.multiple_of(k * AB, AB)
-            bhi[:, pl.ds(to, AB), :] = hi.reshape(rows3 // AB, AB, WIN)
-            blo[:, pl.ds(to, AB), :] = lo.reshape(rows3 // AB, AB, WIN)
+            ahi[k] = hi
+            alo[k] = lo
             return carry
 
-        lax.fori_loop(0, nk, cols_adjoint, 0, unroll=8)
+        lax.fori_loop(0, nk, cols_adjoint, 0, unroll=4)
 
         def rows_adjoint(b, carry):
             start = pl.multiple_of(base + b * AB, AB)
             for w in range(nwin):
-                at = w * (CHUNK // AB) + b
-                p = mm(adj_ref[...], bhi[at])
-                q = mm(adj_ref[:aspan, :], blo[at])
+                at = pl.multiple_of(w * CHUNK + b * AB, AB)
+                p = mm(adj_ref[...], ahi[:, pl.ds(at, AB), :].reshape(nk * AB, WIN))
+                q = mm(adj_ref[:aspan, :], alo[:, pl.ds(at, AB), :].reshape(nk * AB, WIN))
                 z[w, pl.ds(start, aspan), :] += p[:aspan] + p[aspan:] + q
             return carry
 
@@ -316,11 +315,9 @@
             pltpu.VMEM((nk, rows3, WIN), bf16),
             pltpu.VMEM((nk, rows3, WIN), bf16),
             pltpu.VMEM((nk, rows3, WIN), f32),
-            pltpu.VMEM((rows3 // AB, nk * AB, WIN), bf16),
-            pltpu.VMEM((rows3 // AB, nk * AB, WIN), bf16),
             pltpu.VMEM((nwin, eh, WIN), f32),
         ] + [pltpu.VMEM((nk, WIN, WIN), bf16)] * 4 + [pltpu.VMEM((rows3, WIN), f32)],
-        compiler_params=pltpu.CompilerParams(vmem_limit_bytes=60 * 1024 * 1024),
+        compiler_params=pltpu.CompilerParams(vmem_limit_bytes=63 * 1024 * 1024),
     )(inv_sum[None], ext, target, fwd, adj, cvec, avec)
     gradient = fold(grad, reach)
     return resist, gradient

time: 96.6 us -> 93.1 us (0.964)
  Pallas kernels: 81.4 us -> 77.8 us
    pallas_call x1, Pallas kernels: 61.6 us -> 58.1 us  [shards(): pl.pallas_call(functools.partial(tile_kernel, nk, height, breadth, reach)...]
where the time goes in v4:
time: 93.1 us; the launch traced here: 92.1 us
  Pallas kernels  77.8 us (84%)
  local copies, waits for them, and re-layouts  7.33 us (8%)
  other arithmetic  4.3 us (5%)
  between operations  2.08 us (2%)
    pallas_call x1, Pallas kernels, shards(): pl.pallas_call(functools.partial(tile_kernel, nk, height, breadth, reach)...  58.1 us
    pallas_call x1, Pallas kernels, fold(): pl.pallas_call(functools.partial(fold_kernel, reach), out_shape=jax.Shape...  10.6 us
    pallas_call x1, Pallas kernels, widen(): pl.pallas_call(functools.partial(widen_kernel, reach), out_shape=jax.Shap...  9.16 us
    unnamed x7, local copies, waits for them, and re-layouts  3.47 us

profile of v4, /device:TPU:3, one launch (start us, length us, event | category | flops | bytes accessed | tf_op | source)
XLA Modules:
  0.0 92.1 jit_solution(5408061581231027899)
XLA Ops:
  1.3 0.1 pad.11.clone
  1.4 1.3 %compare_select_fusion = (f32[24]{0:T(128)S(1)}, f32[]{:T(128)}) fusion(f32[24]{0:T(128)} %param.9, s32[]{:T(128)} %bitcast), kind=kLoop, calls=%fused_computation.15 | loop fusion | flops 95 | bytes 200 | tf_op jit(solution)/shard_map/jit(_where)/select_n | solution.py:285
  3.3 0.1 pad.6.clone
  3.4 0.8 reduce-precision_convert_fusion
  4.2 0.8 slice.18
  5.0 0.1 rev.3
  5.0 1.4 %pad_maximum_fusion.cvec_ref = f32[24,256]{1,0:T(8,128)} fusion(f32[24,64]{1,0:T(8,128)S(1)} %rev.3, f32[24,1]{1,0:T(8,128)} %bitcast.19, f32[256]{0:T(256)S(1)} %pad.6.clone), kind=kLoop, calls=%fused_computation.8 | loop fusion | flops 12288 | bytes 31840 | tf_op jit(solution)/shard_map/concatenate | solution.py:299
  6.4 1.3 %pad.4.avec_ref = f32[24,256]{1,0:T(8,128)} pad(f32[24,65]{1,0:T(8,128)} %param.8, f32[]{:T(128)} %constant.4.clone.1), padding=0_0x0_191 | pad | bytes 30820 | tf_op jit(solution)/shard_map/jit(_pad)/pad | solution.py:298
  7.8 0.2 convolution_convert_fusion.1
  8.1 0.0 copy-start.2
  8.1 0.8 maximum_maximum_fusion.fwd_ref
  8.9 0.4 convolution_convert_fusion
  9.3 0.4 copy.16
  9.7 0.2 reshape.51
  9.9 0.9 copy.14.adj_ref
  10.8 0.0 copy-done.2
  10.8 9.2 %shard_map.77.mask_ref = f32[576,640]{1,0:T(8,128)S(1)} custom-call(f32[512,512]{1,0:T(8,128)S(1)} %copy-done.2), custom_call_target="tpu_custom_call" | custom-call | tf_op jit(solution)/shard_map/pallas_call | solution.py:244
  20.0 0.0 copy-start
  20.0 1.1 %copy-done = f32[576,640]{1,0:T(8,128)} copy-done((f32[576,640]{1,0:T(8,128)}, f32[576,640]{1,0:T(8,128)S(1)}, u32[]{:S(2)}) %copy-start) | copy-done | bytes 1474584
  21.1 58.1 %shard_map.78 = (f32[512,512]{1,0:T(8,128)}, f32[576,576]{1,0:T(8,128)}) custom-call(f32[1]{0:T(128)} %bitcast.1.scal_ref, f32[576,640]{1,0:T(8,128)} %copy-done, f32[512,512]{1,0:T(8,128)} %target_ref.1, bf16[384,256]{1,0:T(8,128)(2,1)} %maximum_maximum_fusion.fwd_ref, bf16[192,768]{1,0:T(8,128)(2,1)} %copy.14.adj_ref, f32[24,256]{1,0:T(8,128)} %pad_maximum_fusion.cvec_ref, ...), custom_call_target="tpu_custom_call" | custom-call | tf_op jit(solution)/shard_map/pallas_call | solution.py:304
  79.2 0.0 copy-start.1
  79.2 1.4 %copy-done.1 = f32[576,576]{1,0:T(8,128)S(1)} copy-done((f32[576,576]{1,0:T(8,128)S(1)}, f32[576,576]{1,0:T(8,128)}, u32[]{:S(2)}) %copy-start.1) | copy-done | bytes 1327128
  80.6 10.6 %shard_map.79 = f32[512,512]{1,0:T(8,128)S(1)} custom-call(f32[576,576]{1,0:T(8,128)S(1)} %copy-done.1), custom_call_target="tpu_custom_call" | custom-call | tf_op jit(solution)/shard_map/pallas_call | solution.py:258
  91.2 1.0 %copy.19 = f32[512,512]{1,0:T(8,128)} copy(f32[512,512]{1,0:T(8,128)S(1)} %shard_map.79) | data formatting | bytes 2097152
  (7 shorter events, 0.1 us)
Async XLA Ops:
  8.1 2.7 %copy-start.2 = (f32[512,512]{1,0:T(8,128)S(1)}, f32[512,512]{1,0:T(8,128)}, u32[]{:S(2)}) copy-start(f32[512,512]{1,0:T(8,128)} %mask_ref.1) | copy-start | bytes 3145732
  20.0 1.1 %copy-start = (f32[576,640]{1,0:T(8,128)}, f32[576,640]{1,0:T(8,128)S(1)}, u32[]{:S(2)}) copy-start(f32[576,640]{1,0:T(8,128)S(1)} %shard_map.77.mask_ref) | copy-start | bytes 4423684
  79.2 1.4 %copy-start.1 = (f32[576,576]{1,0:T(8,128)S(1)}, f32[576,576]{1,0:T(8,128)}, u32[]{:S(2)}) copy-start(f32[576,576]{1,0:T(8,128)} %get-tuple-element.5.g_ref) | copy-start | bytes 3981316
